TPU v7x, 32 devices: a whole 2x2x4 slice. The times are simulated.
32 devices in a mesh: groups: 2 (over y), expert: 4 (over z), tensor: 4 (over x, core).
Axes of the slice: x: 2, y: 2, z: 4, core: 2. Of those that a mesh axis runs over, the one named last changes fastest.
Arguments:
- tokens: bfloat16 [256, 3072], P(('groups', 'expert'), 'tensor'), parts along dimension 0, may hold values from -6 to 6
- cotangent: bfloat16 [256, 3072], P(('groups', 'expert'), 'tensor'), parts along dimension 0, may hold values from -6 to 6
- route_weights: float32 [256, 2], P(('groups', 'expert')), parts along dimension 0, may hold values from 0.2 to 1
- expert_ids: int32 [256, 2], P(('groups', 'expert')), parts along dimension 0, may hold values from 0 to 3, as said below
- slot_index: int32 [256, 2], P(('groups', 'expert')), parts along dimension 0, may hold values from 0 to 15, as said below
- keep_mask: int32 [256, 2], P(('groups', 'expert')), parts along dimension 0, may hold values from 0 to 1, as said below
- w_gate: bfloat16 [3072, 32768], P(None, ('expert', 'tensor')), may hold values from -0.109375 to 0.109375
- w_up: bfloat16 [3072, 32768], P(None, ('expert', 'tensor')), may hold values from -0.109375 to 0.109375
- w_down: bfloat16 [32768, 3072], P(('expert', 'tensor')), may hold values from -0.0625 to 0.0625
Outputs:
- grad_tokens: bfloat16 [256, 3072], P(('groups', 'expert'), 'tensor'), parts along dimension 0
- grad_down: bfloat16 [65536, 3072], P(('groups', 'expert', 'tensor')), parts along dimension 0
There are 2 independent parts, one for each index of `groups`. A program takes and returns all parts, laid end to end along the dimension named above; an argument that names none is the same for every part. Nothing has to cross between parts.
Inputs may be any that keep to these rules, and one draw needn't show every extreme that they name: `expert_ids`: the two experts of a token differ. `slot_index`: within the 32 rows of one index of expert, the assignments to one expert are numbered 0, 1, 2, ... in the order of tokens and then of k; the number is given where it is under 16, else 16 - 1. `keep_mask`: 1 exactly where the assignment's number within its aligned block of 32 rows is under 16; in every block some expert is full.
All inputs are finite; a program needn't handle non-finite values.
Results may differ from a plain program's by a relative error of at most 0.012.
Values may be sent and summed in bfloat16 or wider, within the bound.
A program may use at most 128 MiB of HBM per device.

v0:
```python
import jax
import jax.numpy as jnp
from jax import lax
from jax.sharding import PartitionSpec as P

EXPERTS = 4


def shards(
    tokens, cotangent, route_weights, expert_ids, slot_index, keep_mask, w_gate, w_up, w_down
):
    tok_rows = tokens.shape[0]
    capacity = tok_rows // 2
    expert_count = lax.axis_size("expert")
    holders = expert_count // EXPERTS
    slots_all = EXPERTS * capacity
    target = jnp.where(keep_mask == 1, expert_ids * capacity + slot_index, slots_all).reshape(-1)
    owners = jnp.full((slots_all + 1,), 2 * tok_rows, jnp.int32)
    owners = owners.at[target].set(jnp.arange(2 * tok_rows, dtype=jnp.int32))[:slots_all]
    token_idx = owners // 2
    full_in, full_cot = (
        lax.all_gather(tokens, "tensor", axis=1, tiled=True),
        lax.all_gather(cotangent, "tensor", axis=1, tiled=True),
    )
    width = full_in.shape[1]
    token_ext = jnp.concatenate([full_in, jnp.zeros((1, width), full_in.dtype)], axis=0)
    weighted = (route_weights[:, :, None] * full_cot[:, None, :].astype(jnp.float32)).astype(
        jnp.bfloat16
    )
    weighted_ext = jnp.concatenate(
        [weighted.reshape(2 * tok_rows, width), jnp.zeros((1, width), jnp.bfloat16)], axis=0
    )
    shape_out = (EXPERTS, capacity, width)
    outgoing_input = jnp.repeat(token_ext[token_idx].reshape(shape_out), holders, axis=0)
    sent_grad = jnp.repeat(weighted_ext[owners].reshape(shape_out), holders, axis=0)
    recv_in, recv_grad = (
        lax.all_to_all(outgoing_input, "expert", split_axis=0, concat_axis=0, tiled=True),
        lax.all_to_all(sent_grad, "expert", split_axis=0, concat_axis=0, tiled=True),
    )
    gate_projection = jnp.einsum("scd,df->scf", recv_in, w_gate, preferred_element_type=jnp.float32)
    up_proj = jnp.einsum("scd,df->scf", recv_in, w_up, preferred_element_type=jnp.float32)
    sigmoid_gate = jax.nn.sigmoid(gate_projection)
    silu_gate = gate_projection * sigmoid_gate
    hidden = (silu_gate * up_proj).astype(jnp.bfloat16)
    grad_down = jnp.einsum(
        "scf,scd->fd", hidden, recv_grad, preferred_element_type=jnp.float32
    ).astype(jnp.bfloat16)
    grad_hidden = jnp.einsum("scd,fd->scf", recv_grad, w_down, preferred_element_type=jnp.float32)
    grad_up = (grad_hidden * silu_gate).astype(jnp.bfloat16)
    grad_gate = (
        grad_hidden * up_proj * sigmoid_gate * (1.0 + gate_projection * (1.0 - sigmoid_gate))
    ).astype(jnp.bfloat16)
    pieces = jnp.einsum("scf,df->scd", grad_gate, w_gate, preferred_element_type=jnp.float32)
    pieces = pieces + jnp.einsum("scf,df->scd", grad_up, w_up, preferred_element_type=jnp.float32)
    pieces = pieces.astype(jnp.bfloat16)
    summed = lax.psum_scatter(pieces, "tensor", scatter_dimension=2, tiled=True).astype(jnp.float32)
    returned = lax.all_to_all(
        summed.astype(jnp.bfloat16), "expert", split_axis=0, concat_axis=0, tiled=True
    ).astype(summed.dtype)
    width = returned.shape[2]
    flat_rows = jnp.sum(returned.reshape(EXPERTS, holders, capacity, width), axis=1).reshape(
        slots_all, width
    )
    combined = jnp.zeros((tok_rows + 1, width), jnp.float32).at[token_idx].add(flat_rows)
    result = combined[:tok_rows]
    return (result.astype(jnp.bfloat16), grad_down)


def solution(mesh):
    in_specs = (
        P(("groups", "expert"), "tensor"),
        P(("groups", "expert"), "tensor"),
        P(("groups", "expert"), None),
        P(("groups", "expert"), None),
        P(("groups", "expert"), None),
        P(("groups", "expert"), None),
        P(None, ("expert", "tensor")),
        P(None, ("expert", "tensor")),
        P(("expert", "tensor"), None),
    )
    out_specs = (P(("groups", "expert"), "tensor"), P(("groups", "expert", "tensor"), None))
    return jax.shard_map(shards, mesh=mesh, in_specs=in_specs, out_specs=out_specs, check_vma=False)
```

profile of v0, /device:TPU:0, one launch (start us, length us, event | category | flops | bytes accessed | tf_op | source)
XLA Modules:
  0.0 116.2 jit_solution(5325843216150107375)
XLA Ops:
  7.2 0.7 compare_select_fusion.2
  7.9 0.1 copy.13
  8.0 0.1 reshape.52
  8.1 0.8 scatter_custom_fusion
  8.9 7.0 %all_gather.7 = bf16[32,3072]{1,0:T(8,128)(2,1)S(1)} all-gather(bf16[32,768]{1,0:T(8,128)(2,1)} %param.9), channel_id=1, replica_groups=mesh['groups'=2,'expert'=4,'tensor'=4] {'tensor'}, dimensions={1}, use_global_device_ids=true | all-gather | bytes 245760 | tf_op jit(solution)/shard_map/all_gather | solution.py:22
  16.0 1.5 %gather_fusion.1 = bf16[64,3072]{1,0:T(8,128)(2,1)} fusion(bf16[33,3072]{1,0:T(8,128)(2,1)S(1)} %concatenate.7, s32[1024]{0:T(1024)S(1)} %pad_clamp_fusion), kind=kCustom, calls=%fused_computation.1 | custom fusion | bytes 786688 | tf_op jit(solution)/shard_map/gather | solution.py:34
  17.5 5.1 %all-to-all-start.1 = ((bf16[4,16,3072]{2,1,0:T(8,128)(2,1)}), bf16[4,16,3072]{2,1,0:T(8,128)(2,1)S(1)}, u32[]{:S(2)}, u32[]{:S(2)}) async-start(bf16[4,16,3072]{2,1,0:T(8,128)(2,1)} %bitcast.3), calls=%async_computation.1 | async-start | bytes 786432 | tf_op jit(solution)/shard_map/all_to_all | solution.py:37
  22.6 0.8 copy.14
  23.4 0.1 mul.47
  23.5 5.8 %all_gather.6 = bf16[32,3072]{1,0:T(8,128)(2,1)S(1)} all-gather(bf16[32,768]{1,0:T(8,128)(2,1)} %param.10), channel_id=1, replica_groups=mesh['groups'=2,'expert'=4,'tensor'=4] {'tensor'}, dimensions={1}, use_global_device_ids=true | all-gather | bytes 245760 | tf_op jit(solution)/shard_map/all_gather | solution.py:23
  29.3 0.2 mul.49
  29.5 0.5 mul.50
  30.0 0.1 multiply_convert_fusion
  30.2 1.5 %gather_fusion = bf16[64,3072]{1,0:T(8,128)(2,1)} fusion(bf16[65,3072]{1,0:T(8,128)(2,1)S(1)} %concatenate.6, s32[1024]{0:T(1024)S(1)} %pad_clamp_fusion.1), kind=kCustom, calls=%fused_computation | custom fusion | bytes 786688 | tf_op jit(solution)/shard_map/gather | solution.py:35
  31.7 3.1 %all-to-all-done.1 = bf16[4,16,3072]{2,1,0:T(8,128)(2,1)S(1)} async-done(((bf16[4,16,3072]{2,1,0:T(8,128)(2,1)}), bf16[4,16,3072]{2,1,0:T(8,128)(2,1)S(1)}, u32[]{:S(2)}, u32[]{:S(2)}) %all-to-all-start.1) | async-done | bytes 393248 | tf_op jit(solution)/shard_map/all_to_all | solution.py:37
  34.8 3.5 %all-to-all-start = ((bf16[4,16,3072]{2,1,0:T(8,128)(2,1)}), bf16[4,16,3072]{2,1,0:T(8,128)(2,1)S(1)}, u32[]{:S(2)}, u32[]{:S(2)}) async-start(bf16[4,16,3072]{2,1,0:T(8,128)(2,1)} %bitcast.1), calls=%async_computation | async-start | bytes 786432 | tf_op jit(solution)/shard_map/all_to_all | solution.py:38
  38.3 0.2 reduce-scatter.2.cloned.1.call-start
  38.5 6.9 %fusion.2 = f32[4,16,2048]{2,1,0:T(8,128)S(1)} fusion(bf16[4,16,3072]{2,1,0:T(8,128)(2,1)S(1)} %all-to-all-done.1, bf16[3072,2048]{1,0:T(8,128)(2,1)} %param.15), kind=kOutput, calls=%fused_computation.7 | convolution fusion | flops 805306368 | bytes 13500416 | tf_op jit(solution)/shard_map/scd,df->scf/dot_general | solution.py:40
  45.4 6.9 %fusion.6 = f32[4,16,2048]{2,1,0:T(8,128)S(1)} fusion(bf16[4,16,3072]{2,1,0:T(8,128)(2,1)S(1)} %all-to-all-done.1, bf16[3072,2048]{1,0:T(8,128)(2,1)} %param.16), kind=kOutput, calls=%fused_computation.11 | convolution fusion | flops 805306368 | bytes 13500416 | tf_op jit(solution)/shard_map/scd,df->scf/dot_general | solution.py:41
  52.2 0.0 all-to-all-done
  52.3 0.0 slice-start
  52.3 0.0 slice-start.1
  52.3 8.6 %fusion.8 = f32[4,16,2048]{2,1,0:T(8,128)S(1)} fusion(bf16[4,16,3072]{2,1,0:T(8,128)(2,1)S(1)} %all-to-all-done, bf16[2048,3072]{1,0:T(8,128)(2,1)} %param.17), kind=kOutput, calls=%fused_computation.13 | convolution fusion | flops 805306368 | bytes 13500416 | tf_op jit(solution)/shard_map/scd,fd->scf/dot_general | solution.py:48
  60.9 0.0 slice-start.2
  60.9 8.6 %fusion = f32[4,16,3072]{2,1,0:T(8,128)S(1)} fusion(bf16[3072,2048]{1,0:T(8,128)(2,1)} %param.15, f32[4,16,2048]{2,1,0:T(8,128)S(1)} %fusion.2, f32[4,16,2048]{2,1,0:T(8,128)S(1)} %fusion.8, f32[4,16,2048]{2,1,0:T(8,128)S(1)} %fusion.6), kind=kOutput, calls=%fused_computation.5 | convolution fusion | flops 806617088 | bytes 14942208 | tf_op jit(solution)/shard_map/scf,df->scd/dot_general | solution.py:53
  69.6 4.7 %fusion.13 = bf16[4,16,3072]{2,1,0:T(8,128)(2,1)} fusion(f32[4,16,3072]{2,1,0:T(8,128)S(1)} %fusion, bf16[3072,2048]{1,0:T(8,128)(2,1)S(1)} %bitcast.31, f32[4,16,2048]{2,1,0:T(8,128)S(1)} %fusion.8, f32[4,16,2048]{2,1,0:T(8,128)S(1)} %fusion.2), kind=kOutput, calls=%fused_computation.16 | convolution fusion | flops 806486016 | bytes 14811136 | tf_op jit(solution)/shard_map/scf,df->scd/dot_general | solution.py:54
  74.3 0.0 reduce-scatter.2.cloned.1.call-update
  74.3 22.2 %reduce-scatter.2.cloned.1.call-done = bf16[4,16,768]{2,1,0:T(8,128)(2,1)} async-done(((bf16[4,16,3072]{2,1,0:T(8,128)(2,1)}), bf16[4,16,768]{2,1,0:T(8,128)(2,1)}) %reduce-scatter.2.cloned.1.call-update) | async-done | bytes 98320 | tf_op jit(solution)/shard_map/reduce_scatter | solution.py:56
  96.5 4.6 %all-to-all-start.2 = ((bf16[4,16,768]{2,1,0:T(8,128)(2,1)}), bf16[4,16,768]{2,1,0:T(8,128)(2,1)S(1)}, u32[]{:S(2)}, u32[]{:S(2)}) async-start(bf16[4,16,768]{2,1,0:T(8,128)(2,1)} %reduce-scatter.2.cloned.1.call-done), calls=%async_computation.3 | async-start | bytes 196608 | tf_op jit(solution)/shard_map/all_to_all | solution.py:57
  101.1 6.6 %bitcast_convert_fusion = bf16[2048,3072]{1,0:T(8,128)(2,1)} fusion(bf16[4,16,3072]{2,1,0:T(8,128)(2,1)S(1)} %all-to-all-done, f32[4,16,2048]{2,1,0:T(8,128)S(1)} %fusion.6, f32[4,16,2048]{2,1,0:T(8,128)S(1)} %fusion.2), kind=kOutput, calls=%fused_computation.4 | convolution fusion | flops 812384256 | bytes 14024704 | tf_op jit(solution)/shard_map/scf,scd->fd/dot_general | solution.py:45
  107.7 1.0 scatter_custom_fusion.1
  108.8 0.6 slice.17
  (12 shorter events, 0.1 us)
Async XLA Ops:
  17.5 17.3 %all-to-all-start.1 = ((bf16[4,16,3072]{2,1,0:T(8,128)(2,1)}), bf16[4,16,3072]{2,1,0:T(8,128)(2,1)S(1)}, u32[]{:S(2)}, u32[]{:S(2)}) async-start(bf16[4,16,3072]{2,1,0:T(8,128)(2,1)} %bitcast.3), calls=%async_computation.1 | async-start | bytes 786432 | tf_op jit(solution)/shard_map/all_to_all | solution.py:37
  34.8 17.4 %all-to-all-start = ((bf16[4,16,3072]{2,1,0:T(8,128)(2,1)}), bf16[4,16,3072]{2,1,0:T(8,128)(2,1)S(1)}, u32[]{:S(2)}, u32[]{:S(2)}) async-start(bf16[4,16,3072]{2,1,0:T(8,128)(2,1)} %bitcast.1), calls=%async_computation | async-start | bytes 786432 | tf_op jit(solution)/shard_map/all_to_all | solution.py:38
  38.3 58.2 %reduce-scatter.2.cloned.1.call-start = ((), (), s32[]{:S(2)}) async-start(), calls=%async_computation.4 | async-start | bytes 491520 | tf_op jit(solution)/shard_map/reduce_scatter | solution.py:56
  52.3 17.3 %slice-start = ((s8[12582912]{0:T(1024)(128)(4,1)}), s8[4194304]{0:T(1024)(128)(4,1)S(1)}, s32[]{:S(2)}) async-start(s8[12582912]{0:T(1024)(128)(4,1)} %bitcast.30), calls=%async_computation.5 | async-start | bytes 8388608
  52.3 17.3 %slice-start.1 = ((s8[12582912]{0:T(1024)(128)(4,1)}), s8[4194304]{0:T(1024)(128)(4,1)S(1)}, s32[]{:S(2)}) async-start(s8[12582912]{0:T(1024)(128)(4,1)} %bitcast.30), calls=%async_computation.6 | async-start | bytes 8388608
  60.9 8.7 %slice-start.2 = ((s8[12582912]{0:T(1024)(128)(4,1)}), s8[4194304]{0:T(1024)(128)(4,1)S(1)}, s32[]{:S(2)}) async-start(s8[12582912]{0:T(1024)(128)(4,1)} %bitcast.30), calls=%async_computation.7 | async-start | bytes 8388608
  96.5 11.2 %all-to-all-start.2 = ((bf16[4,16,768]{2,1,0:T(8,128)(2,1)}), bf16[4,16,768]{2,1,0:T(8,128)(2,1)S(1)}, u32[]{:S(2)}, u32[]{:S(2)}) async-start(bf16[4,16,768]{2,1,0:T(8,128)(2,1)} %reduce-scatter.2.cloned.1.call-done), calls=%async_computation.3 | async-start | bytes 196608 | tf_op jit(solution)/shard_map/all_to_all | solution.py:57
Sparse Core Ops, SparseCore 0:
  74.5 21.9 reduce-scatter.1
where the time goes:
time: 117 us; the launch traced here: 116 us
  matrix products  42.3 us (36%)
  waiting for transfers between devices  25.2 us (22%)
  between operations  14.2 us (12%)
  starting transfers between devices  13.4 us (11%)
  blocking collectives  12.9 us (11%)
  local copies, waits for them, and re-layouts  6.33 us (5%)
  other arithmetic  1.89 us (2%)
    reduce_scatter x1, waiting for transfers between devices, shards(): lax.psum_scatter(pieces, 'tensor', scatter_dimension=2, tiled=True)  22.2 us
    dot_general x1, matrix products, shards(): jnp.einsum('scf,df->scd', grad_gate, w_gate, preferred_element_type=jnp.f...  8.64 us
    dot_general x1, matrix products, shards(): jnp.einsum('scd,fd->scf', recv_grad, w_down, preferred_element_type=jnp.f...  8.64 us
    all_gather x1, blocking collectives, shards(): lax.all_gather(tokens, 'tensor', axis=1, tiled=True)  7.05 us
    dot_general x1, matrix products, shards(): jnp.einsum('scd,df->scf', recv_in, w_up, preferred_element_type=jnp.float32)  6.87 us
    dot_general x1, matrix products, shards(): jnp.einsum('scd,df->scf', recv_in, w_gate, preferred_element_type=jnp.flo...  6.87 us
    dot_general x1, matrix products, shards(): jnp.einsum('scf,scd->fd', hidden, recv_grad, preferred_element_type=jnp.f...  6.63 us
    all_gather x1, blocking collectives, shards(): lax.all_gather(cotangent, 'tensor', axis=1, tiled=True)  5.82 us
  transfers between devices with their start and end apart: 4, of which 2 were waited for; matrix products, arithmetic and copies ran while one was open for 20% of the time, Pallas kernels for 0%

commit v1 on v0

v1 whole, which is shorter than its diff:
```python
import functools

import jax
import jax.numpy as jnp
from jax import lax
from jax.experimental import pallas as pl
from jax.experimental.pallas import tpu as pltpu
from jax.sharding import PartitionSpec as P

EXPERTS = 4
F32 = jnp.float32
BF16 = jnp.bfloat16
NT = (((1,), (1,)), ((), ()))
TN = (((0,), (0,)), ((), ()))


def matmul(a, b, dims=(((1,), (0,)), ((), ()))):
    return lax.dot_general(a, b, dims, preferred_element_type=F32)


def layer_kernel(
    n_exp, n_ten, cap, chunk,
    tok_ref, cot_ref, rw_ref, ids_ref, slot_ref, keep_ref, wg_hbm, wu_hbm, wd_hbm,
    grad_ref, hidden_ref, weighted_ref,
    wg, wu, wd, outgoing, gath, rows_in, gg, gu, piece, red, ret_out, ret_in,
    w_sem, a_send, a_recv, b_send, b_recv, c_send, c_recv, r_send, r_recv, z_send, z_recv,
):
    holders = n_exp // EXPERTS
    chips = n_ten // 2
    tok_rows, width = tok_ref.shape
    ff = wg.shape[1]
    rows = n_exp * cap
    e = lax.axis_index("expert")
    t = lax.axis_index("tensor")
    x = t // 2
    c = t % 2

    w_copies = []
    for i in range(ff // chunk):
        part = pl.ds(i * chunk, chunk)
        trio = [
            pltpu.make_async_copy(wg_hbm.at[:, part], wg.at[:, part], w_sem.at[0, i]),
            pltpu.make_async_copy(wu_hbm.at[:, part], wu.at[:, part], w_sem.at[1, i]),
            pltpu.make_async_copy(wd_hbm.at[part, :], wd.at[part, :], w_sem.at[2, i]),
        ]
        for copy in trio:
            copy.start()
        w_copies.append(trio)

    barrier = pltpu.get_barrier_semaphore()
    for k in range(1, n_exp):
        pl.semaphore_signal(
            barrier, inc=1, device_id={"expert": lax.rem(e + k, n_exp)},
            device_id_type=pl.DeviceIdType.MESH,
        )
    for k in range(1, n_ten):
        pl.semaphore_signal(
            barrier, inc=1, device_id={"tensor": lax.rem(t + k, n_ten)},
            device_id_type=pl.DeviceIdType.MESH,
        )

    ids, slot, keep = ids_ref[...], slot_ref[...], keep_ref[...]
    rw = rw_ref[...]
    target = jnp.where(keep == 1, ids * cap + slot, -1)
    row = lax.broadcasted_iota(jnp.int32, (EXPERTS * cap, tok_rows), 0)
    first, second = row == target[0:1, :], row == target[1:2, :]
    zero = jnp.zeros((), F32)
    select = (jnp.where(first, 1.0, zero) + jnp.where(second, 1.0, zero)).astype(BF16)
    row_weight = jnp.sum(
        jnp.where(first, rw[0:1, :], zero) + jnp.where(second, rw[1:2, :], zero),
        axis=1, keepdims=True,
    )
    disp = matmul(select, tok_ref[...]).astype(BF16)
    wgt = (row_weight * matmul(select, cot_ref[...])).astype(BF16)
    for i in range(EXPERTS):
        outgoing[i, 0:cap, :] = disp[i * cap : (i + 1) * cap]
        outgoing[i, cap : 2 * cap, :] = wgt[i * cap : (i + 1) * cap]
    gath[t, e] = outgoing[e // holders]
    pl.semaphore_wait(barrier, n_exp - 1 + n_ten - 1)

    def remote(src, dst, send, recv, expert, tensor):
        return pltpu.make_async_remote_copy(
            src_ref=src, dst_ref=dst, send_sem=send, recv_sem=recv,
            device_id={"expert": expert, "tensor": tensor},
            device_id_type=pl.DeviceIdType.MESH,
        )

    sent = []

    def send(*args):
        copy = remote(*args)
        copy.start()
        sent.append(copy)

    for k in range(1, n_exp):
        dest = lax.rem(e + k, n_exp)
        send(
            outgoing.at[dest // holders], gath.at[t, e], a_send.at[k], a_recv.at[k], dest, t
        )
    mate = x * 2 + (1 - c)
    for k in range(n_exp):
        s = lax.rem(e - k + n_exp, n_exp)
        block = gath.at[t, s]
        if k:
            remote(block, block, a_send.at[k], a_recv.at[k], s, t).wait_recv()
        for dx in range(1, chips):
            send(
                block, block, b_send.at[dx, k], b_recv.at[dx, k], e,
                lax.rem(x + dx, chips) * 2 + c,
            )
        send(block, block, b_send.at[0, k], b_recv.at[0, k], e, mate)
    for k in range(n_exp):
        s = lax.rem(e - k + n_exp, n_exp)
        for dx in range(1, chips):
            block = gath.at[lax.rem(x - dx + chips, chips) * 2 + c, s]
            remote(
                block, block, b_send.at[dx, k], b_recv.at[dx, k], e, mate
            ).wait_recv()
            send(block, block, c_send.at[dx, k], c_recv.at[dx, k], e, mate)
    for k in range(n_exp):
        s = lax.rem(e - k + n_exp, n_exp)
        block = gath.at[mate, s]
        remote(block, block, b_send.at[0, k], b_recv.at[0, k], e, mate).wait_recv()
        for dx in range(1, chips):
            block = gath.at[lax.rem(x - dx + chips, chips) * 2 + (1 - c), s]
            remote(block, block, c_send.at[dx, k], c_recv.at[dx, k], e, mate).wait_recv()
    for j in range(n_ten):
        for s in range(n_exp):
            place = (slice(s * cap, (s + 1) * cap), slice(j * width, (j + 1) * width))
            rows_in[place] = gath[j, s, 0:cap, :]
            weighted_ref[place] = gath[j, s, cap : 2 * cap, :]

    for i in range(ff // chunk):
        part = slice(i * chunk, (i + 1) * chunk)
        w_copies[i][0].wait()
        w_copies[i][1].wait()
        w_copies[i][2].wait()
        gate = matmul(rows_in[...], wg[:, part])
        up = matmul(rows_in[...], wu[:, part])
        back = matmul(weighted_ref[...], wd[part, :], NT)
        sigmoid = jax.nn.sigmoid(gate)
        silu = gate * sigmoid
        hidden_ref[:, part] = (silu * up).astype(BF16)
        gu[:, part] = (back * silu).astype(BF16)
        gg[:, part] = (back * up * sigmoid * (1.0 + gate * (1.0 - sigmoid))).astype(BF16)

    order = [(dx, dc) for dx in range(1, chips) for dc in range(2)] + [(0, 1), (0, 0)]
    for j, (dx, dc) in enumerate(order):
        dest = lax.rem(x + dx, chips) * 2 + (c if dc == 0 else 1 - c)
        part = pl.ds(pl.multiple_of(dest * width, width), width)
        value = matmul(gg[...], wg[part, :], NT) + matmul(gu[...], wu[part, :], NT)
        piece[j] = value.astype(BF16)
        if j < n_ten - 1:
            send(piece.at[j], red.at[j], r_send.at[j], r_recv.at[j], e, dest)
    total = piece[n_ten - 1].astype(F32)
    for j in range(n_ten - 1):
        remote(piece.at[j], red.at[j], r_send.at[j], r_recv.at[j], e, mate).wait_recv()
        total = total + red[j].astype(F32)
    ret_out[...] = total.astype(BF16).reshape(n_exp, cap, width)
    for k in range(1, n_exp):
        dest = lax.rem(e + k, n_exp)
        send(ret_out.at[dest], ret_in.at[e], z_send.at[k], z_recv.at[k], dest, t)
    ret_in[e] = ret_out[e]
    for k in range(1, n_exp):
        s = lax.rem(e - k + n_exp, n_exp)
        remote(ret_out.at[s], ret_in.at[s], z_send.at[k], z_recv.at[k], s, t).wait_recv()

    row = lax.broadcasted_iota(jnp.int32, (rows, tok_rows), 0)
    owner = row >> ((cap * holders).bit_length() - 1)
    row = owner * cap + (row & (cap - 1))
    first, second = row == target[0:1, :], row == target[1:2, :]
    select = (jnp.where(first, 1.0, zero) + jnp.where(second, 1.0, zero)).astype(BF16)
    grad_ref[...] = matmul(select, ret_in[...].reshape(rows, width), TN).astype(BF16)
    for copy in sent:
        copy.wait_send()


def shards(
    tokens, cotangent, route_weights, expert_ids, slot_index, keep_mask, w_gate, w_up, w_down
):
    tok_rows, width = tokens.shape
    cap = tok_rows // 2
    n_exp, n_ten = lax.axis_size("expert"), lax.axis_size("tensor")
    chips = n_ten // 2
    rows = n_exp * cap
    depth, ff = w_gate.shape
    chunk = min(512, ff)
    dma = pltpu.SemaphoreType.DMA
    vmem = pl.BlockSpec(memory_space=pltpu.VMEM)
    hbm = pl.BlockSpec(memory_space=pl.ANY)
    grad_tokens, hidden, weighted = pl.pallas_call(
        functools.partial(layer_kernel, n_exp, n_ten, cap, chunk),
        out_shape=(
            jax.ShapeDtypeStruct((tok_rows, width), BF16),
            jax.ShapeDtypeStruct((rows, ff), BF16),
            jax.ShapeDtypeStruct((rows, depth), BF16),
        ),
        in_specs=[vmem] * 6 + [hbm] * 3,
        out_specs=(vmem, vmem, vmem),
        scratch_shapes=[
            pltpu.VMEM((depth, ff), BF16),
            pltpu.VMEM((depth, ff), BF16),
            pltpu.VMEM((ff, depth), BF16),
            pltpu.VMEM((EXPERTS, 2 * cap, width), BF16),
            pltpu.VMEM((n_ten, n_exp, 2 * cap, width), BF16),
            pltpu.VMEM((rows, depth), BF16),
            pltpu.VMEM((rows, ff), BF16),
            pltpu.VMEM((rows, ff), BF16),
            pltpu.VMEM((n_ten, rows, width), BF16),
            pltpu.VMEM((n_ten, rows, width), BF16),
            pltpu.VMEM((n_exp, cap, width), BF16),
            pltpu.VMEM((n_exp, cap, width), BF16),
            dma((3, ff // chunk)),
            dma((n_exp,)),
            dma((n_exp,)),
            dma((chips, n_exp)),
            dma((chips, n_exp)),
            dma((chips, n_exp)),
            dma((chips, n_exp)),
            dma((n_ten,)),
            dma((n_ten,)),
            dma((n_exp,)),
            dma((n_exp,)),
        ],
        compiler_params=pltpu.CompilerParams(
            collective_id=0, has_side_effects=True, vmem_limit_bytes=56 * 2**20
        ),
        cost_estimate=pl.CostEstimate(
            flops=10 * rows * depth * ff,
            bytes_accessed=6 * depth * ff,
            transcendentals=rows * ff,
        ),
    )(
        tokens, cotangent, route_weights.T, expert_ids.T, slot_index.T, keep_mask.T,
        w_gate, w_up, w_down,
    )
    grad_down = lax.dot_general(hidden, weighted, TN, preferred_element_type=F32).astype(BF16)
    return grad_tokens, grad_down


def solution(mesh):
    in_specs = (
        P(("groups", "expert"), "tensor"),
        P(("groups", "expert"), "tensor"),
        P(("groups", "expert"), None),
        P(("groups", "expert"), None),
        P(("groups", "expert"), None),
        P(("groups", "expert"), None),
        P(None, ("expert", "tensor")),
        P(None, ("expert", "tensor")),
        P(("expert", "tensor"), None),
    )
    out_specs = (P(("groups", "expert"), "tensor"), P(("groups", "expert", "tensor"), None))
    return jax.shard_map(shards, mesh=mesh, in_specs=in_specs, out_specs=out_specs, check_vma=False)
```

time: 117 us -> 50.6 us (0.43)
  Pallas kernels: 0 us -> 39.8 us
  matrix products: 42.3 us -> 9.32 us
  waiting for transfers between devices: 25.2 us -> 0 us
  between operations: 14.2 us -> 0.65 us
  starting transfers between devices: 13.4 us -> 0 us
  blocking collectives: 12.9 us -> 0 us
  local copies, waits for them, and re-layouts: 6.33 us -> 0.62 us
  other arithmetic: 1.89 us -> 0 us
    pallas_call x0 -> x1, Pallas kernels: none -> 39.8 us  [shards(): pl.pallas_call(functools.partial(layer_kernel, n_exp, n_ten, cap, chunk),...]
    dot_general x6 -> x1, matrix products: 42.3 us -> 9.32 us  [shards(): lax.dot_general(hidden, weighted, TN, preferred_element_type=F32)]
    reduce_scatter x1 -> x0, waiting for transfers between devices: 22.2 us -> none  [shards(): lax.psum_scatter(pieces, 'tensor', scatter_dimension=2, tiled=True)]
    all_to_all x3 -> x0, starting transfers between devices: 13.1 us -> none  [the longest x1 5.09 us: shards(): lax.all_to_all(outgoing_input, 'expert', split_axis=0, concat_axis=0, til...]
    all_gather x2 -> x0, blocking collectives: 12.9 us -> none  [the longest x1 7.05 us: shards(): lax.all_gather(tokens, 'tensor', axis=1, tiled=True)]
    gather x2 -> x0, local copies, waits for them, and re-layouts: 3.06 us -> none  [the longest x1 1.53 us: shards(): token_ext[token_idx].reshape(shape_out)]
    all_to_all x3 -> x0, waiting for transfers between devices: 3.06 us -> none  [the longest x1 3.05 us: shards(): lax.all_to_all(outgoing_input, 'expert', split_axis=0, concat_axis=0, til...]
  transfers between devices with their start and end apart: 4 -> 0, of which waited for: 2 -> 0; matrix products, arithmetic and copies ran while one was open for 20% -> 0% of each run, Pallas kernels for 0% -> 0%
where the time goes in v1:
time: 50.6 us; the launch traced here: 50.4 us
  Pallas kernels  39.8 us (79%)
  matrix products  9.32 us (18%)
  between operations  0.65 us (1%)
  local copies, waits for them, and re-layouts  0.62 us (1%)
    pallas_call x1, Pallas kernels, shards(): pl.pallas_call(functools.partial(layer_kernel, n_exp, n_ten, cap, chunk),...  39.8 us
    dot_general x1, matrix products, shards(): lax.dot_general(hidden, weighted, TN, preferred_element_type=F32)  9.32 us

profile of v1, /device:TPU:0, one launch (start us, length us, event | category | flops | bytes accessed | tf_op | source)
XLA Modules:
  0.0 50.4 jit_solution(5259048896984197110)
XLA Ops:
  0.6 39.8 %shard_map.104 = (bf16[32,768]{1,0:T(8,128)(2,1)}, bf16[64,2048]{1,0:T(8,128)(2,1)}, bf16[64,3072]{1,0:T(8,128)(2,1)}) custom-call(bf16[32,768]{1,0:T(8,128)(2,1)} %tok_ref.1, bf16[32,768]{1,0:T(8,128)(2,1)} %cot_ref.1, f32[2,32]{1,0:T(2,128)} %bitcast.6, s32[2,32]{1,0:T(2,128)} %bitcast.7, s32[2,32]{1,0:T(2,128)} %bitcast.8, s32[2,32]{1,0:T(2,128)} %bitcast.9, ...), custom_call_target="tpu_custom_call" | custom-call | flops 4026531840 | bytes 37748736 | tf_op jit(solution)/shard_map/pallas_call | solution.py:191
  40.4 0.0 copy-start
  40.4 9.3 %convolution_convert_fusion = bf16[2048,3072]{1,0:T(8,128)(2,1)} fusion(bf16[64,2048]{1,0:T(8,128)(2,1)} %get-tuple-element.6, bf16[64,3072]{1,0:T(8,128)(2,1)} %get-tuple-element.7), kind=kOutput, calls=%fused_computation | convolution fusion | flops 811597824 | bytes 13238272 | tf_op jit(solution)/shard_map/dot_general | solution.py:237
  49.7 0.0 copy-done
  49.7 0.6 %copy.12 = bf16[32,768]{1,0:T(8,128)(2,1)} copy(bf16[32,768]{1,0:T(8,128)(2,1)S(1)} %copy-done) | data formatting | bytes 98304
Async XLA Ops:
  40.4 9.3 %copy-start = (bf16[32,768]{1,0:T(8,128)(2,1)S(1)}, bf16[32,768]{1,0:T(8,128)(2,1)}, u32[]{:S(2)}) copy-start(bf16[32,768]{1,0:T(8,128)(2,1)} %get-tuple-element.10) | copy-start | bytes 147460

commit v2 on v1

--- a/solution.py
+++ b/solution.py
@@ -21,8 +21,8 @@
 def layer_kernel(
     n_exp, n_ten, cap, chunk,
     tok_ref, cot_ref, rw_ref, ids_ref, slot_ref, keep_ref, wg_hbm, wu_hbm, wd_hbm,
-    grad_ref, hidden_ref, weighted_ref,
-    wg, wu, wd, outgoing, gath, rows_in, gg, gu, piece, red, ret_out, ret_in,
+    ret_ref, hidden_ref, weighted_ref,
+    wg, wu, wd, outgoing, gath, gate_acc, up_acc, back_acc, gg, gu, piece, red, ret_out, ret_in,
     w_sem, a_send, a_recv, b_send, b_recv, c_send, c_recv, r_send, r_recv, z_send, z_recv,
 ):
     holders = n_exp // EXPERTS
@@ -35,13 +35,17 @@
     x = t // 2
     c = t % 2
 
+    arrivals = [(dx, dc) for dx in range(chips) for dc in range(2)]
+    blocks = [
+        lax.rem(x - dx + chips, chips) * 2 + (c if dc == 0 else 1 - c) for dx, dc in arrivals
+    ]
     w_copies = []
-    for i in range(ff // chunk):
-        part = pl.ds(i * chunk, chunk)
+    for i, block in enumerate(blocks):
+        part = pl.ds(pl.multiple_of(block * width, width), width)
         trio = [
-            pltpu.make_async_copy(wg_hbm.at[:, part], wg.at[:, part], w_sem.at[0, i]),
-            pltpu.make_async_copy(wu_hbm.at[:, part], wu.at[:, part], w_sem.at[1, i]),
-            pltpu.make_async_copy(wd_hbm.at[part, :], wd.at[part, :], w_sem.at[2, i]),
+            pltpu.make_async_copy(wg_hbm.at[part, :], wg.at[part, :], w_sem.at[0, i]),
+            pltpu.make_async_copy(wu_hbm.at[part, :], wu.at[part, :], w_sem.at[1, i]),
+            pltpu.make_async_copy(wd_hbm.at[:, part], wd.at[:, part], w_sem.at[2, i]),
         ]
         for copy in trio:
             copy.start()
@@ -109,10 +113,40 @@
                 lax.rem(x + dx, chips) * 2 + c,
             )
         send(block, block, b_send.at[0, k], b_recv.at[0, k], e, mate)
+
+    def project(i):
+        for copy in w_copies[i]:
+            copy.wait()
+        part = pl.ds(pl.multiple_of(blocks[i] * width, width), width)
+        both = gath[blocks[i]]
+        rows_in = both[:, 0:cap, :].reshape(rows, width)
+        weighted = both[:, cap : 2 * cap, :].reshape(rows, width)
+        weighted_ref[:, part] = weighted
+        for j in range(ff // chunk):
+            cols = slice(j * chunk, (j + 1) * chunk)
+            gate = matmul(rows_in, wg[part, cols])
+            up = matmul(rows_in, wu[part, cols])
+            back = matmul(weighted, wd[cols, part], NT)
+            if i:
+                gate = gate + gate_acc[:, cols]
+                up = up + up_acc[:, cols]
+                back = back + back_acc[:, cols]
+            if i < n_ten - 1:
+                gate_acc[:, cols] = gate
+                up_acc[:, cols] = up
+                back_acc[:, cols] = back
+            else:
+                sigmoid = jax.nn.sigmoid(gate)
+                silu = gate * sigmoid
+                hidden_ref[:, cols] = (silu * up).astype(BF16)
+                gu[:, cols] = (back * silu).astype(BF16)
+                gg[:, cols] = (back * up * sigmoid * (1.0 + gate * (1.0 - sigmoid))).astype(BF16)
+
+    project(0)
     for k in range(n_exp):
         s = lax.rem(e - k + n_exp, n_exp)
         for dx in range(1, chips):
-            block = gath.at[lax.rem(x - dx + chips, chips) * 2 + c, s]
+            block = gath.at[blocks[2 * dx], s]
             remote(
                 block, block, b_send.at[dx, k], b_recv.at[dx, k], e, mate
             ).wait_recv()
@@ -121,28 +155,14 @@
         s = lax.rem(e - k + n_exp, n_exp)
         block = gath.at[mate, s]
         remote(block, block, b_send.at[0, k], b_recv.at[0, k], e, mate).wait_recv()
-        for dx in range(1, chips):
-            block = gath.at[lax.rem(x - dx + chips, chips) * 2 + (1 - c), s]
+    project(1)
+    for dx in range(1, chips):
+        project(2 * dx)
+        for k in range(n_exp):
+            s = lax.rem(e - k + n_exp, n_exp)
+            block = gath.at[blocks[2 * dx + 1], s]
             remote(block, block, c_send.at[dx, k], c_recv.at[dx, k], e, mate).wait_recv()
-    for j in range(n_ten):
-        for s in range(n_exp):
-            place = (slice(s * cap, (s + 1) * cap), slice(j * width, (j + 1) * width))
-            rows_in[place] = gath[j, s, 0:cap, :]
-            weighted_ref[place] = gath[j, s, cap : 2 * cap, :]
-
-    for i in range(ff // chunk):
-        part = slice(i * chunk, (i + 1) * chunk)
-        w_copies[i][0].wait()
-        w_copies[i][1].wait()
-        w_copies[i][2].wait()
-        gate = matmul(rows_in[...], wg[:, part])
-        up = matmul(rows_in[...], wu[:, part])
-        back = matmul(weighted_ref[...], wd[part, :], NT)
-        sigmoid = jax.nn.sigmoid(gate)
-        silu = gate * sigmoid
-        hidden_ref[:, part] = (silu * up).astype(BF16)
-        gu[:, part] = (back * silu).astype(BF16)
-        gg[:, part] = (back * up * sigmoid * (1.0 + gate * (1.0 - sigmoid))).astype(BF16)
+        project(2 * dx + 1)
 
     order = [(dx, dc) for dx in range(1, chips) for dc in range(2)] + [(0, 1), (0, 0)]
     for j, (dx, dc) in enumerate(order):
@@ -165,14 +185,29 @@
         s = lax.rem(e - k + n_exp, n_exp)
         remote(ret_out.at[s], ret_in.at[s], z_send.at[k], z_recv.at[k], s, t).wait_recv()
 
-    row = lax.broadcasted_iota(jnp.int32, (rows, tok_rows), 0)
-    owner = row >> ((cap * holders).bit_length() - 1)
-    row = owner * cap + (row & (cap - 1))
-    first, second = row == target[0:1, :], row == target[1:2, :]
-    select = (jnp.where(first, 1.0, zero) + jnp.where(second, 1.0, zero)).astype(BF16)
-    grad_ref[...] = matmul(select, ret_in[...].reshape(rows, width), TN).astype(BF16)
+    ret_ref[...] = ret_in[...]
     for copy in sent:
         copy.wait_send()
+
+
+def down_kernel(
+    cap, holders, ids_ref, slot_ref, keep_ref, ret_ref, hidden_ref, weighted_ref,
+    grad_ref, out_ref,
+):
+    out_ref[...] = matmul(hidden_ref[...], weighted_ref[...], TN).astype(BF16)
+
+    @pl.when(pl.program_id(0) == 0)
+    def _():
+        n_exp, _, width = ret_ref.shape
+        rows = n_exp * cap
+        target = jnp.where(keep_ref[...] == 1, ids_ref[...] * cap + slot_ref[...], -1)
+        row = lax.broadcasted_iota(jnp.int32, (rows, target.shape[1]), 0)
+        owner = row >> ((cap * holders).bit_length() - 1)
+        row = owner * cap + (row & (cap - 1))
+        first, second = row == target[0:1, :], row == target[1:2, :]
+        zero = jnp.zeros((), F32)
+        select = (jnp.where(first, 1.0, zero) + jnp.where(second, 1.0, zero)).astype(BF16)
+        grad_ref[...] = matmul(select, ret_ref[...].reshape(rows, width), TN).astype(BF16)
 
 
 def shards(
@@ -185,13 +220,14 @@
     rows = n_exp * cap
     depth, ff = w_gate.shape
     chunk = min(512, ff)
+    meta = (expert_ids.T, slot_index.T, keep_mask.T)
     dma = pltpu.SemaphoreType.DMA
     vmem = pl.BlockSpec(memory_space=pltpu.VMEM)
     hbm = pl.BlockSpec(memory_space=pl.ANY)
-    grad_tokens, hidden, weighted = pl.pallas_call(
+    returned, hidden, weighted = pl.pallas_call(
         functools.partial(layer_kernel, n_exp, n_ten, cap, chunk),
         out_shape=(
-            jax.ShapeDtypeStruct((tok_rows, width), BF16),
+            jax.ShapeDtypeStruct((n_exp, cap, width), BF16),
             jax.ShapeDtypeStruct((rows, ff), BF16),
             jax.ShapeDtypeStruct((rows, depth), BF16),
         ),
@@ -203,14 +239,16 @@
             pltpu.VMEM((ff, depth), BF16),
             pltpu.VMEM((EXPERTS, 2 * cap, width), BF16),
             pltpu.VMEM((n_ten, n_exp, 2 * cap, width), BF16),
-            pltpu.VMEM((rows, depth), BF16),
+            pltpu.VMEM((rows, ff), F32),
+            pltpu.VMEM((rows, ff), F32),
+            pltpu.VMEM((rows, ff), F32),
             pltpu.VMEM((rows, ff), BF16),
             pltpu.VMEM((rows, ff), BF16),
             pltpu.VMEM((n_ten, rows, width), BF16),
             pltpu.VMEM((n_ten, rows, width), BF16),
             pltpu.VMEM((n_exp, cap, width), BF16),
             pltpu.VMEM((n_exp, cap, width), BF16),
-            dma((3, ff // chunk)),
+            dma((3, n_ten)),
             dma((n_exp,)),
             dma((n_exp,)),
             dma((chips, n_exp)),
@@ -231,10 +269,32 @@
             transcendentals=rows * ff,
         ),
     )(
-        tokens, cotangent, route_weights.T, expert_ids.T, slot_index.T, keep_mask.T,
+        tokens, cotangent, route_weights.T, *meta,
         w_gate, w_up, w_down,
     )
-    grad_down = lax.dot_general(hidden, weighted, TN, preferred_element_type=F32).astype(BF16)
+    tile = min(512, ff)
+    grad_tokens, grad_down = pl.pallas_call(
+        functools.partial(down_kernel, cap, n_exp // EXPERTS),
+        out_shape=(
+            jax.ShapeDtypeStruct((tok_rows, width), BF16),
+            jax.ShapeDtypeStruct((ff, depth), BF16),
+        ),
+        grid=(ff // tile,),
+        in_specs=[pl.BlockSpec((2, tok_rows), lambda i: (0, 0))] * 3
+        + [
+            pl.BlockSpec((n_exp, cap, width), lambda i: (0, 0, 0)),
+            pl.BlockSpec((rows, tile), lambda i: (0, i)),
+            pl.BlockSpec((rows, depth), lambda i: (0, 0)),
+        ],
+        out_specs=(
+            pl.BlockSpec((tok_rows, width), lambda i: (0, 0)),
+            pl.BlockSpec((tile, depth), lambda i: (i, 0)),
+        ),
+        compiler_params=pltpu.CompilerParams(vmem_limit_bytes=32 * 2**20),
+        cost_estimate=pl.CostEstimate(
+            flops=2 * rows * depth * ff, bytes_accessed=2 * depth * ff, transcendentals=0
+        ),
+    )(*meta, returned, hidden, weighted)
     return grad_tokens, grad_down
 
 

time: 50.6 us -> 47.6 us (0.941)
  matrix products: 9.32 us -> 0 us
  Pallas kernels: 39.8 us -> 43.8 us
  local copies, waits for them, and re-layouts: 0.62 us -> 2.84 us
    dot_general x1 -> x0, matrix products: 9.32 us -> none  [shards(): lax.dot_general(hidden, weighted, TN, preferred_element_type=F32)]
    pallas_call x0 -> x1, Pallas kernels: none -> 6.58 us  [shards(): pl.pallas_call(functools.partial(down_kernel, cap, n_exp // EXPERTS), out...]
    pallas_call x1, Pallas kernels: 39.8 us -> 37.2 us  [shards(): pl.pallas_call(functools.partial(layer_kernel, n_exp, n_ten, cap, chunk),...]
    unnamed x3 -> x12, local copies, waits for them, and re-layouts: 0.62 us -> 2.84 us
where the time goes in v2:
time: 47.6 us; the launch traced here: 47.3 us
  Pallas kernels  43.8 us (92%)
  local copies, waits for them, and re-layouts  2.84 us (6%)
  between operations  0.7 us (1%)
    pallas_call x1, Pallas kernels, shards(): pl.pallas_call(functools.partial(layer_kernel, n_exp, n_ten, cap, chunk),...  37.2 us
    pallas_call x1, Pallas kernels, shards(): pl.pallas_call(functools.partial(down_kernel, cap, n_exp // EXPERTS), out...  6.58 us
    unnamed x12, local copies, waits for them, and re-layouts  2.84 us

profile of v2, /device:TPU:0, one launch (start us, length us, event | category | flops | bytes accessed | tf_op | source)
XLA Modules:
  0.0 47.3 jit_solution(3137585144473978100)
XLA Ops:
  0.6 0.0 copy-start
  0.6 0.0 copy-start.1
  0.7 0.0 copy-start.2
  0.7 37.2 %shard_map.104 = (bf16[4,16,768]{2,1,0:T(8,128)(2,1)}, bf16[64,2048]{1,0:T(8,128)(2,1)}, bf16[64,3072]{1,0:T(8,128)(2,1)}) custom-call(bf16[32,768]{1,0:T(8,128)(2,1)} %tok_ref.1, bf16[32,768]{1,0:T(8,128)(2,1)} %cot_ref.1, f32[2,32]{1,0:T(2,128)} %bitcast.10, s32[2,32]{1,0:T(2,128)} %bitcast.4, s32[2,32]{1,0:T(2,128)} %bitcast.6, s32[2,32]{1,0:T(2,128)} %bitcast.8, ...), custom_call_target="tpu_custom_call" | custom-call | flops 4026531840 | bytes 37748736 | tf_op jit(solution)/shard_map/pallas_call | solution.py:227
  37.9 0.0 copy-done
  37.9 0.0 copy-done.1
  37.9 0.0 copy-done.2
  37.9 0.0 copy-start.3
  37.9 1.0 %copy-done.3 = bf16[64,3072]{1,0:T(8,128)(2,1)S(1)} copy-done((bf16[64,3072]{1,0:T(8,128)(2,1)S(1)}, bf16[64,3072]{1,0:T(8,128)(2,1)}, u32[]{:S(2)}) %copy-start.3) | copy-done | bytes 393240
  38.9 0.0 copy-start.4
  38.9 0.9 %copy-done.4 = bf16[64,2048]{1,0:T(8,128)(2,1)S(1)} copy-done((bf16[64,2048]{1,0:T(8,128)(2,1)S(1)}, bf16[64,2048]{1,0:T(8,128)(2,1)}, u32[]{:S(2)}) %copy-start.4) | copy-done | bytes 262168
  39.9 0.0 copy-start.5
  39.9 0.9 %copy-done.5 = bf16[4,16,768]{2,1,0:T(8,128)(2,1)S(1)} copy-done((bf16[4,16,768]{2,1,0:T(8,128)(2,1)S(1)}, bf16[4,16,768]{2,1,0:T(8,128)(2,1)}, u32[]{:S(2)}) %copy-start.5) | copy-done | bytes 98328
  40.8 6.6 %shard_map.105 = (bf16[32,768]{1,0:T(8,128)(2,1)}, bf16[2048,3072]{1,0:T(8,128)(2,1)}) custom-call(s32[2,32]{1,0:T(2,128)S(1)} %bitcast.5, s32[2,32]{1,0:T(2,128)S(1)} %bitcast.7, s32[2,32]{1,0:T(2,128)S(1)} %bitcast.9, bf16[4,16,768]{2,1,0:T(8,128)(2,1)S(1)} %copy-done.5, bf16[64,2048]{1,0:T(8,128)(2,1)S(1)} %copy-done.4, bf16[64,3072]{1,0:T(8,128)(2,1)S(1)} %copy-done.3), custom_call_target="tpu_custom_call" | custom-call | flops 805306368 | bytes 12582912 | tf_op jit(solution)/shard_map/pallas_call | solution.py:276
Async XLA Ops:
  0.6 37.3 %copy-start = (s32[32,2]{0,1:T(2,128)S(1)}, s32[32,2]{0,1:T(2,128)}, u32[]{:S(2)}) copy-start(s32[32,2]{0,1:T(2,128)} %param.12) | copy-start | bytes 772
  0.6 37.3 %copy-start.1 = (s32[32,2]{0,1:T(2,128)S(1)}, s32[32,2]{0,1:T(2,128)}, u32[]{:S(2)}) copy-start(s32[32,2]{0,1:T(2,128)} %param.13) | copy-start | bytes 772
  0.7 37.3 %copy-start.2 = (s32[32,2]{0,1:T(2,128)S(1)}, s32[32,2]{0,1:T(2,128)}, u32[]{:S(2)}) copy-start(s32[32,2]{0,1:T(2,128)} %param.14) | copy-start | bytes 772
  37.9 1.0 %copy-start.3 = (bf16[64,3072]{1,0:T(8,128)(2,1)S(1)}, bf16[64,3072]{1,0:T(8,128)(2,1)}, u32[]{:S(2)}) copy-start(bf16[64,3072]{1,0:T(8,128)(2,1)} %get-tuple-element.7.weighted_ref) | copy-start | bytes 1179652
  38.9 0.9 %copy-start.4 = (bf16[64,2048]{1,0:T(8,128)(2,1)S(1)}, bf16[64,2048]{1,0:T(8,128)(2,1)}, u32[]{:S(2)}) copy-start(bf16[64,2048]{1,0:T(8,128)(2,1)} %get-tuple-element.6.hidden_ref) | copy-start | bytes 786436
  39.9 0.9 %copy-start.5 = (bf16[4,16,768]{2,1,0:T(8,128)(2,1)S(1)}, bf16[4,16,768]{2,1,0:T(8,128)(2,1)}, u32[]{:S(2)}) copy-start(bf16[4,16,768]{2,1,0:T(8,128)(2,1)} %get-tuple-element.5.ret_ref) | copy-start | bytes 294916

commit v3 on v2

--- a/solution.py
+++ b/solution.py
@@ -21,9 +21,9 @@
 def layer_kernel(
     n_exp, n_ten, cap, chunk,
     tok_ref, cot_ref, rw_ref, ids_ref, slot_ref, keep_ref, wg_hbm, wu_hbm, wd_hbm,
-    ret_ref, hidden_ref, weighted_ref,
-    wg, wu, wd, outgoing, gath, gate_acc, up_acc, back_acc, gg, gu, piece, red, ret_out, ret_in,
-    w_sem, a_send, a_recv, b_send, b_recv, c_send, c_recv, r_send, r_recv, z_send, z_recv,
+    ret_ref, hidden_out, weighted_out,
+    hidden_ref, weighted_ref, wg, wu, wd, outgoing, gath, gate_acc, up_acc, back_acc, gg, gu, piece, red, ret_out, ret_in,
+    w_sem, o_sem, a_send, a_recv, b_send, b_recv, c_send, c_recv, r_send, r_recv, z_send, z_recv,
 ):
     holders = n_exp // EXPERTS
     chips = n_ten // 2
@@ -163,6 +163,12 @@
             block = gath.at[blocks[2 * dx + 1], s]
             remote(block, block, c_send.at[dx, k], c_recv.at[dx, k], e, mate).wait_recv()
         project(2 * dx + 1)
+    out_copies = [
+        pltpu.make_async_copy(hidden_ref, hidden_out, o_sem.at[0]),
+        pltpu.make_async_copy(weighted_ref, weighted_out, o_sem.at[1]),
+    ]
+    for copy in out_copies:
+        copy.start()
 
     order = [(dx, dc) for dx in range(1, chips) for dc in range(2)] + [(0, 1), (0, 0)]
     for j, (dx, dc) in enumerate(order):
@@ -188,6 +194,8 @@
     ret_ref[...] = ret_in[...]
     for copy in sent:
         copy.wait_send()
+    for copy in out_copies:
+        copy.wait()
 
 
 def down_kernel(
@@ -232,8 +240,10 @@
             jax.ShapeDtypeStruct((rows, depth), BF16),
         ),
         in_specs=[vmem] * 6 + [hbm] * 3,
-        out_specs=(vmem, vmem, vmem),
+        out_specs=(vmem, hbm, hbm),
         scratch_shapes=[
+            pltpu.VMEM((rows, ff), BF16),
+            pltpu.VMEM((rows, depth), BF16),
             pltpu.VMEM((depth, ff), BF16),
             pltpu.VMEM((depth, ff), BF16),
             pltpu.VMEM((ff, depth), BF16),
@@ -249,6 +259,7 @@
             pltpu.VMEM((n_exp, cap, width), BF16),
             pltpu.VMEM((n_exp, cap, width), BF16),
             dma((3, n_ten)),
+            dma((2,)),
             dma((n_exp,)),
             dma((n_exp,)),
             dma((chips, n_exp)),
@@ -290,7 +301,7 @@
             pl.BlockSpec((tok_rows, width), lambda i: (0, 0)),
             pl.BlockSpec((tile, depth), lambda i: (i, 0)),
         ),
-        compiler_params=pltpu.CompilerParams(vmem_limit_bytes=32 * 2**20),
+        compiler_params=pltpu.CompilerParams(vmem_limit_bytes=56 * 2**20),
         cost_estimate=pl.CostEstimate(
             flops=2 * rows * depth * ff, bytes_accessed=2 * depth * ff, transcendentals=0
         ),

time: 47.6 us -> 45.5 us (0.956)
  local copies, waits for them, and re-layouts: 2.84 us -> 0 us
  Pallas kernels: 43.8 us -> 44.7 us
    unnamed x12 -> x0, local copies, waits for them, and re-layouts: 2.84 us -> none
    pallas_call x1, Pallas kernels: 6.58 us -> 7.7 us  [shards(): pl.pallas_call(functools.partial(down_kernel, cap, n_exp // EXPERTS), out...]
where the time goes in v3:
time: 45.5 us; the launch traced here: 45.3 us
  Pallas kernels  44.7 us (98%)
  between operations  0.64 us (1%)
    pallas_call x1, Pallas kernels, shards(): pl.pallas_call(functools.partial(layer_kernel, n_exp, n_ten, cap, chunk),...  37 us
    pallas_call x1, Pallas kernels, shards(): pl.pallas_call(functools.partial(down_kernel, cap, n_exp // EXPERTS), out...  7.7 us

profile of v3, /device:TPU:0, one launch (start us, length us, event | category | flops | bytes accessed | tf_op | source)
XLA Modules:
  0.0 45.3 jit_solution(5187709878846827147)
XLA Ops:
  0.6 37.0 %shard_map.104 = (bf16[4,16,768]{2,1,0:T(8,128)(2,1)}, bf16[64,2048]{1,0:T(8,128)(2,1)}, bf16[64,3072]{1,0:T(8,128)(2,1)}) custom-call(bf16[32,768]{1,0:T(8,128)(2,1)} %tok_ref.1, bf16[32,768]{1,0:T(8,128)(2,1)} %cot_ref.1, f32[2,32]{1,0:T(2,128)} %bitcast.4, s32[2,32]{1,0:T(2,128)} %bitcast.5, s32[2,32]{1,0:T(2,128)} %bitcast.7, s32[2,32]{1,0:T(2,128)} %bitcast.9, ...), custom_call_target="tpu_custom_call" | custom-call | flops 4026531840 | bytes 37748736 | tf_op jit(solution)/shard_map/pallas_call | solution.py:235
  37.6 7.7 %shard_map.105 = (bf16[32,768]{1,0:T(8,128)(2,1)}, bf16[2048,3072]{1,0:T(8,128)(2,1)}) custom-call(s32[2,32]{1,0:T(2,128)} %bitcast.6, s32[2,32]{1,0:T(2,128)} %bitcast.8, s32[2,32]{1,0:T(2,128)} %bitcast.10, bf16[4,16,768]{2,1,0:T(8,128)(2,1)} %get-tuple-element.5.ret_ref, bf16[64,2048]{1,0:T(8,128)(2,1)} %get-tuple-element.6.hidden_ref, ...), custom_call_target="tpu_custom_call" | custom-call | flops 805306368 | bytes 12582912 | tf_op jit(solution)/shard_map/pallas_call | solution.py:287
